TPU v7x, 32 devices: a whole 2x2x4 slice. The times are simulated.
32 devices in a mesh: gx: 8 (over y, x, core), gy: 4 (over z).
Axes of the slice: x: 2, y: 2, z: 4, core: 2. Of those that a mesh axis runs over, the one named last changes fastest.
Arguments:
- water_head: float32 [256, 128, 128], P('gx', 'gy'), may hold values from -4 to 4
- conductivity: float32 [256, 128, 128], P('gx', 'gy'), may hold values from 1 to 8
- recharge: float32 [256, 128, 128], P('gx', 'gy'), may hold values from -4 to 4
Outputs:
- next_head: float32 [256, 128, 128], P('gx', 'gy')
All inputs are finite; a program needn't handle non-finite values.
Results may differ from a plain program's by a relative error of at most 0.008.
Values sent between devices are 32-bit elements; how exact they have to be, the bound alone decides.
A program may use at most 64 MiB of HBM per device.

v0:
```python
import functools

import jax
import jax.numpy as jnp
from jax import lax
from jax.experimental import pallas as pl
from jax.experimental.pallas import tpu as pltpu
from jax.sharding import PartitionSpec as P

COEF_Z = 8
COEF_X = 5120
COEF_Y = 5120
ROWS = 8
PARTS = 4
MESH = pl.DeviceIdType.MESH


def inverse(x):
    return pl.reciprocal(x, approx=True, full_range=False)


def link(coef, one_side, other_side):
    return (coef * one_side * other_side) * inverse(one_side + other_side)


def blocks(start, stop, size, body, carry):
    return lax.fori_loop(start // size, stop // size, lambda block, carry: body(block * size, carry), carry)


def plane(i, size):
    start = i * size
    return pl.ds(start if isinstance(i, int) else pl.multiple_of(start, size), size)


def pivots(links, share):
    result = []
    for behind, ahead in zip(links[:-1], links[1:]):
        if not result:
            top = 1.0 + behind * share
            bottom = top + ahead
            scale = inverse(bottom)
            result.append(scale)
        else:
            top = bottom + behind * top
            below, bottom = bottom, top + ahead * bottom
            scale = inverse(bottom)
            result.append(below * scale)
    return result, top * scale


def factor_segment(links, cells, rows, fwd_p, bwd_p, near, far, gains, carry=None):
    size = 4

    def body(keep, i, carry):
        states, stores = [], []
        for (s, g), (p_ref, first, way) in zip(carry, ((fwd_p, i, 1), (bwd_p, cells - 1 - i, -1))):
            edge = first + (way < 0)
            beside = [links[plane(edge + way * u, rows)] for u in range(size + 1)]
            parts, s = pivots(beside, s)
            for u, p in enumerate(parts):
                at = plane(first + way * u, rows)
                g = g * (beside[u] * p)
                stores.append((p_ref, at, p))
                if keep:
                    stores += [(near, at, beside[u + 1] * p), (far, at, g)]
            states.append((s, g))
        for ref, at, value in stores:
            ref[at] = value
        return tuple(states)

    half = cells // 2
    if carry is None:
        ones = jnp.ones((rows, 128), jnp.float32)
        return blocks(0, half, size, functools.partial(body, False), ((ones, ones), (ones, ones)))
    (_, g_f), (_, g_b) = blocks(half, cells, size, functools.partial(body, True), carry)
    gains[0] = near[plane(0, rows)]
    gains[1] = g_b
    gains[2] = g_f
    gains[3] = near[plane(cells - 1, rows)]


def sweep_values(rhs, links, cells, rows, fwd_p, bwd_p, value, ends):
    size = 4

    def body(keep, i, carry):
        y_f, y_b = carry
        stores = []
        for u in range(size):
            j = cells - 1 - i - u
            here, there = plane(i + u, rows), plane(j, rows)
            p_f, p_b = fwd_p[here], bwd_p[there]
            y_f = rhs[here] * p_f + (links[here] * p_f) * y_f
            y_b = rhs[there] * p_b + (links[plane(j + 1, rows)] * p_b) * y_b
            stores += [(here, y_f), (there, y_b)]
        if keep:
            for at, y in stores:
                value[at] = y
        return y_f, y_b

    half = cells // 2
    zeros = jnp.zeros((rows, 128), jnp.float32)
    carry = blocks(0, half, size, functools.partial(body, False), (zeros, zeros))
    y_f, y_b = blocks(half, cells, size, functools.partial(body, True), carry)
    ends[0] = y_b
    ends[1] = y_f


def back_substitute(before, after, cells, rows, near, far, value, unroll, store):
    def lap(block, carry):
        low, high = carry
        lows, highs = [], []
        for u in range(unroll):
            i = block * unroll + u
            here, there = plane(i, rows), plane(cells - 1 - i, rows)
            low = (value[here] + far[here] * after) + near[here] * low
            high = (value[there] + far[there] * before) + near[there] * high
            lows.append(low)
            highs.append(high)
        store(block, lows, highs)
        return low, high

    lax.fori_loop(0, cells // 2 // unroll, lap, (before, after))


class Reduced:
    def __init__(self, axis, rows, refs):
        self.axis, self.count, self.me = axis, lax.axis_size(axis), lax.axis_index(axis)
        self.owners = min(self.count, rows // ROWS)
        self.rows = rows // self.owners
        self.stride = self.count // self.owners
        self.mine = lax.rem(self.me, self.stride) == 0
        self.group = self.me // self.stride
        (self.gains, self.ends, self.all_gains, self.all_ends, self.relation, self.reply, self.sides) = refs[:7]
        (self.gain_send, self.gain_recv, self.end_send, self.end_recv, self.reply_send, self.reply_recv) = refs[7:]

    def copy(self, src, dst, send, recv, to):
        return pltpu.make_async_remote_copy(
            src_ref=src, dst_ref=dst, send_sem=send, recv_sem=recv,
            device_id={self.axis: to}, device_id_type=MESH,
        )

    def to_owner(self, o, source, everyone, send, recv):
        return self.copy(
            source.at[:, pl.ds(o * self.rows, self.rows), :], everyone.at[self.me],
            send.at[o], recv.at[self.me], o * self.stride,
        )

    def spread(self, source, everyone, send, recv):
        for o in range(self.owners):

            @pl.when(self.me != o * self.stride)
            def _():
                self.to_owner(o, source, everyone, send, recv).start()

            @pl.when(self.me == o * self.stride)
            def _():
                everyone[o * self.stride] = source[:, o * self.rows : (o + 1) * self.rows, :]

    def send_gains(self):
        self.spread(self.gains, self.all_gains, self.gain_send, self.gain_recv)

    def send_ends(self):
        self.spread(self.ends, self.all_ends, self.end_send, self.end_recv)

    def arrived(self, everyone, recv):
        for d in range(1, self.count):
            k = lax.rem(self.me + d, self.count)
            self.copy(everyone.at[k], everyone.at[k], recv.at[k], recv.at[k], k).wait_recv()

    def factor(self):
        @pl.when(self.mine)
        def _():
            self.arrived(self.all_gains, self.gain_recv)
            gain = jnp.zeros((self.rows, 128), jnp.float32)
            for k in range(self.count):
                head_west, head_east = self.all_gains[k, 0], self.all_gains[k, 1]
                tail_west, tail_east = self.all_gains[k, 2], self.all_gains[k, 3]
                scale = inverse(1.0 - head_west * gain)
                beta, gamma = head_east * scale, tail_west * gain
                self.relation[k, 0], self.relation[k, 1] = scale, beta
                self.relation[k, 2], self.relation[k, 3] = gamma, gain
                gain = tail_east + gamma * beta

    def reply_copy(self, k):
        return self.copy(
            self.reply.at[k], self.sides.at[self.group],
            self.reply_send.at[k], self.reply_recv.at[self.group], k,
        )

    def solve(self):
        @pl.when(self.mine)
        def _():
            self.arrived(self.all_ends, self.end_recv)
            value = jnp.zeros((self.rows, 128), jnp.float32)
            alphas, values = [], []
            for k in range(self.count):
                values.append(value)
                scale, gamma = self.relation[k, 0], self.relation[k, 2]
                head_west, tail_west = self.all_gains[k, 0], self.all_gains[k, 2]
                alpha = (self.all_ends[k, 0] + head_west * value) * scale
                value = (self.all_ends[k, 1] + tail_west * value) + gamma * alpha
                alphas.append(alpha)
            after = jnp.zeros((self.rows, 128), jnp.float32)
            for k in reversed(range(self.count)):
                self.reply[k, 1] = after
                after = alphas[k] + self.relation[k, 1] * after
                self.reply[k, 0] = values[k] + self.relation[k, 3] * after
            for d in range(1, self.count):
                self.reply_copy(lax.rem(self.me + d, self.count)).start()
            self.sides[self.group] = self.reply[self.me]

    def result(self):
        for o in range(self.owners):

            @pl.when(self.me != o * self.stride)
            def _():
                self.copy(
                    self.sides.at[o], self.sides.at[o], self.reply_recv.at[o], self.reply_recv.at[o],
                    o * self.stride,
                ).wait_recv()

        whole = (self.owners * self.rows, 128)
        return self.sides[:, 0].reshape(whole), self.sides[:, 1].reshape(whole)

    def drain(self):
        for o in range(self.owners):

            @pl.when(self.me != o * self.stride)
            def _():
                self.to_owner(o, self.gains, self.all_gains, self.gain_send, self.gain_recv).wait_send()
                self.to_owner(o, self.ends, self.all_ends, self.end_send, self.end_recv).wait_send()

        @pl.when(self.mine)
        def _():
            for d in range(1, self.count):
                self.reply_copy(lax.rem(self.me + d, self.count)).wait_send()


def reduced_scratch(count, rows):
    owners = min(count, rows // ROWS)
    part = rows // owners
    dma = pltpu.SemaphoreType.DMA
    return [
        pltpu.VMEM((4, rows, 128), jnp.float32),
        pltpu.VMEM((2, rows, 128), jnp.float32),
        pltpu.VMEM((count, 4, part, 128), jnp.float32),
        pltpu.VMEM((count, 2, part, 128), jnp.float32),
        pltpu.VMEM((count, 4, part, 128), jnp.float32),
        pltpu.VMEM((count, 2, part, 128), jnp.float32),
        pltpu.VMEM((owners, 2, part, 128), jnp.float32),
        dma((owners,)), dma((count,)), dma((owners,)), dma((count,)), dma((count,)), dma((owners,)),
    ]


def kernel(X, Y, h_in, c_in, q_in, out, *scratch):
    Z = 128
    chunks = X * Y // 128
    (stage_x, stage_y, halo_x, halo_y, halo_send, halo_recv, force, link_x, link_y, link_z) = scratch[:10]
    fwd_x, bwd_x, near_x, far_x, value_x, fwd_y, bwd_y, near_y, far_y, value_y = scratch[10:20]
    first, up_z, piv_z, lag_z, lead_z, val_z, low_z, h, c, q, load_sem = scratch[20:31]
    along_x = Reduced("gx", Y, scratch[31:44])
    along_y = Reduced("gy", X, scratch[44:57])
    nx, ny, me_x, me_y = along_x.count, along_y.count, along_x.me, along_y.me

    part = X * Y // PARTS
    loads = [
        pltpu.make_async_copy(src.at[pl.ds(m * part, part)], dst.at[pl.ds(m * part, part)], load_sem.at[k, m])
        for k, (src, dst) in enumerate(((h_in, h), (c_in, c), (q_in, q)))
        for m in range(PARTS)
    ]
    for load in loads:
        load.start()
    barrier = pltpu.get_barrier_semaphore()
    for d in range(1, nx):
        pl.semaphore_signal(barrier, inc=1, device_id={"gx": lax.rem(me_x + d, nx)}, device_id_type=MESH)
    for d in range(1, ny):
        pl.semaphore_signal(barrier, inc=1, device_id={"gy": lax.rem(me_y + d, ny)}, device_id_type=MESH)

    for load in loads[: 2 * PARTS]:
        load.wait()

    def column(j):
        return pl.ds(j, X, stride=Y)

    for side, (i, j) in enumerate(((0, 0), (X - 1, Y - 1))):
        stage_x[side, 0], stage_x[side, 1] = h[plane(i, Y)], c[plane(i, Y)]
        stage_y[side, 0], stage_y[side, 1] = h[column(j), :], c[column(j), :]

    for load in loads[2 * PARTS :]:
        load.wait()

    def along_first(i, carry):
        head, cond, flux = carry
        stores = []
        for u in range(4):
            here, ahead = plane(i + u, Y), plane(jnp.minimum(i + u + 1, X - 1), Y)
            head_next, cond_next = h[ahead], c[ahead]
            east = link(COEF_X, cond, cond_next)
            flux_next = east * (head_next - head)
            stores += [(link_x, plane(i + u + 1, Y), east), (force, here, 2.0 * (flux_next - flux) + q[here])]
            head, cond, flux = head_next, cond_next, flux_next
        for ref, at, value in stores:
            ref[at] = value
        return head, cond, flux

    blocks(0, X, 4, along_first, (h[plane(0, Y)], c[plane(0, Y)], jnp.zeros((Y, 128), jnp.float32)))

    pl.semaphore_wait(barrier, nx - 1 + ny - 1)

    halos = []
    for a, (axis, me, count, stage, halo) in enumerate(
        (("gx", me_x, nx, stage_x, halo_x), ("gy", me_y, ny, stage_y, halo_y))
    ):
        for side in (0, 1):
            to = me - 1 if side == 0 else me + 1
            inside = me > 0 if side == 0 else me < count - 1
            send = pltpu.make_async_remote_copy(
                src_ref=stage.at[side], dst_ref=halo.at[1 - side],
                send_sem=halo_send.at[2 * a + side], recv_sem=halo_recv.at[2 * a + 1 - side],
                device_id={axis: to}, device_id_type=MESH,
            )
            take = pltpu.make_async_remote_copy(
                src_ref=stage.at[side], dst_ref=halo.at[side],
                send_sem=halo_send.at[2 * a + side], recv_sem=halo_recv.at[2 * a + side],
                device_id={axis: to}, device_id_type=MESH,
            )
            halos.append((inside, send, take))

            @pl.when(inside)
            def _():
                send.start()

            @pl.when(jnp.logical_not(inside))
            def _():
                halo[side] = jnp.zeros((2,) + halo.shape[2:], jnp.float32)

    inner = lax.broadcasted_iota(jnp.int32, (X, 128), 1) < Z - 1

    def depth_and_second(j, carry):
        head, cond, flux = carry
        stores = []
        for u in range(4):
            ahead = jnp.minimum(j + u + 1, Y - 1)
            head_next, cond_next = h[column(ahead), :], c[column(ahead), :]
            old = force[column(j + u), :]
            up = jnp.where(inner, link(COEF_Z, cond, pltpu.roll(cond, Z - 1, 1)), 0.0)
            rise = up * (pltpu.roll(head, Z - 1, 1) - head)
            north = link(COEF_Y, cond, cond_next)
            flux_next = north * (head_next - head)
            total = old + 2.0 * ((rise - pltpu.roll(rise, 1, 1)) + (flux_next - flux))
            stores.append((link_z, plane(j + u, X), up))
            stores.append((link_y, plane(j + u + 1, X), north))
            stores.append((force, column(j + u), total))
            head, cond, flux = head_next, cond_next, flux_next
        for ref, at, value in stores:
            ref[at, :] = value
        return head, cond, flux

    blocks(0, Y, 4, depth_and_second, (h[column(0), :], c[column(0), :], jnp.zeros((X, 128), jnp.float32)))

    for inside, _, take in halos:

        @pl.when(inside)
        def _():
            take.wait_recv()

    low = link(COEF_X, halo_x[0, 1], c[plane(0, Y)])
    high = link(COEF_X, halo_x[1, 1], c[plane(X - 1, Y)])
    link_x[plane(0, Y)], link_x[plane(X, Y)] = low, high
    force[plane(0, Y)] += 2.0 * (low * (halo_x[0, 0] - h[plane(0, Y)]))
    force[plane(X - 1, Y)] += 2.0 * (high * (halo_x[1, 0] - h[plane(X - 1, Y)]))
    low = link(COEF_Y, halo_y[0, 1], c[column(0), :])
    high = link(COEF_Y, halo_y[1, 1], c[column(Y - 1), :])
    link_y[plane(0, X)], link_y[plane(Y, X)] = low, high
    force[column(0), :] += 2.0 * (low * (halo_y[0, 0] - h[column(0), :]))
    force[column(Y - 1), :] += 2.0 * (high * (halo_y[1, 0] - h[column(Y - 1), :]))

    segment_x = (link_x, X, Y, fwd_x, bwd_x, near_x, far_x, along_x.gains)
    factor_segment(*segment_x, factor_segment(*segment_x))
    along_x.send_gains()
    sweep_values(force, link_x, X, Y, fwd_x, bwd_x, value_x, along_x.ends)
    along_x.send_ends()

    segment_y = (link_y, Y, X, fwd_y, bwd_y, near_y, far_y, along_y.gains)
    along_x.factor()
    halfway = factor_segment(*segment_y)
    along_x.solve()
    factor_segment(*segment_y, halfway)
    along_y.send_gains()

    before, after = along_x.result()

    def store_first(block, lows, highs):
        for u in range(4):
            i = block * 4 + u
            first[pl.ds(i, Y, stride=X), :] = lows[u]
            first[pl.ds(X - 1 - i, Y, stride=X), :] = highs[u]

    back_substitute(before, after, X, Y, near_x, far_x, value_x, 4, store_first)

    sweep_values(first, link_y, Y, X, fwd_y, bwd_y, value_y, along_y.ends)
    along_y.send_ends()
    along_y.factor()

    def turn_links(k, carry):
        for u in range(2):
            up_z[pl.ds(chunks + k + u, Z, stride=chunks), :] = link_z[plane(k + u, 128)].T
        return carry

    ones, zeros = (jnp.full((chunks, 128), v, jnp.float32) for v in (1.0, 0.0))
    up_z[plane(0, chunks)] = zeros
    blocks(0, chunks, 2, turn_links, 0)
    half = Z // 2

    def factor_z(i, carry):
        states, stores = [], []
        for s, (first_cell, way) in zip(carry, ((i, 1), (Z - 1 - i, -1))):
            edge = first_cell + (way < 0)
            beside = [up_z[plane(edge + way * u, chunks)] for u in range(9)]
            parts, s = pivots(beside, s)
            for u, p in enumerate(parts):
                at = plane(first_cell + way * u, chunks)
                stores += [(piv_z, at, p), (lag_z, at, beside[u] * p), (lead_z, at, beside[u + 1] * p)]
            states.append(s)
        for ref, at, value in stores:
            ref[at] = value
        return tuple(states)

    carry = blocks(0, half // 2, 8, factor_z, (ones, ones))
    along_y.solve()
    s_f, s_b = blocks(half // 2, half, 8, factor_z, carry)
    middle = inverse(s_f + s_b * lead_z[plane(half - 1, chunks)])
    before, after = along_y.result()
    per_chunk = 128 // X

    def store_second(block, lows, highs):
        val_z[pl.ds(block, Z, stride=chunks), :] = jnp.concatenate(lows, 0).T
        val_z[pl.ds(chunks - 1 - block, Z, stride=chunks), :] = jnp.concatenate(highs[::-1], 0).T

    back_substitute(before, after, Y, X, near_y, far_y, value_y, per_chunk, store_second)

    def sweep_z(i, carry):
        y_f, y_b = carry
        stores = []
        for u in range(8):
            here, there = plane(i + u, chunks), plane(Z - 1 - i - u, chunks)
            y_f = val_z[here] * piv_z[here] + lag_z[here] * y_f
            y_b = val_z[there] * piv_z[there] + lag_z[there] * y_b
            stores += [(here, y_f), (there, y_b)]
        for at, y in stores:
            low_z[at] = y
        return y_f, y_b

    y_f, y_b = blocks(0, half, 8, sweep_z, (zeros, zeros))
    below = (y_f + lead_z[plane(half - 1, chunks)] * y_b) * middle
    above = y_b + lead_z[plane(half, chunks)] * below

    def back_z(i, carry):
        low, high = carry
        stores = []
        for u in range(8):
            stores += [(plane(half - 1 - i - u, chunks), low), (plane(half + i + u, chunks), high)]
            nearer = plane(jnp.maximum(half - 2 - i - u, 0), chunks)
            farther = plane(jnp.minimum(half + 1 + i + u, Z - 1), chunks)
            low = low_z[nearer] + lead_z[nearer] * low
            high = low_z[farther] + lead_z[farther] * high
        for at, value in stores:
            out[at] = value
        return low, high

    blocks(0, half, 8, back_z, (below, above))

    for inside, send, _ in halos:

        @pl.when(inside)
        def _():
            send.wait_send()

    along_x.drain()
    along_y.drain()

def finish(X, Y, delta, h, out):
    chunks, per_chunk = X * Y // 128, 128 // X

    def write(k, carry):
        stores = []
        for u in range(2):
            lines = delta[pl.ds(k + u, 128, stride=chunks), :].T
            for part in range(per_chunk):
                at = pl.ds((k + u) * per_chunk + part, X, stride=Y)
                stores.append((at, h[at, :] + lines[part * X : (part + 1) * X]))
        for at, value in stores:
            out[at, :] = value
        return carry

    blocks(0, chunks, 2, write, 0)


def per_device(water_head, conductivity, recharge):
    X, Y, Z = water_head.shape
    nx, ny = lax.axis_size("gx"), lax.axis_size("gy")

    def vmem(*shape):
        return pltpu.VMEM(shape, jnp.float32)

    cells = X * Y
    chunks = cells // 128
    scratch = [
        vmem(2, 2, Y, Z), vmem(2, 2, X, Z), vmem(2, 2, Y, Z), vmem(2, 2, X, Z),
        pltpu.SemaphoreType.DMA((4,)), pltpu.SemaphoreType.DMA((4,)),
        vmem(cells, Z), vmem(cells + Y, Z), vmem(cells + X, Z), vmem(cells, Z),
    ]
    scratch += [vmem(cells, Z) for _ in range(11)] + [vmem(cells + chunks, Z)] + [vmem(cells, Z) for _ in range(8)] + [pltpu.SemaphoreType.DMA((3, PARTS))]
    scratch += reduced_scratch(nx, Y) + reduced_scratch(ny, X)
    flat = [array.reshape(cells, Z) for array in (water_head, conductivity, recharge)]
    delta = pl.pallas_call(
        functools.partial(kernel, X, Y),
        out_shape=jax.ShapeDtypeStruct((cells, Z), jnp.float32),
        in_specs=[pl.BlockSpec(memory_space=pl.ANY)] * 3,
        out_specs=pl.BlockSpec(memory_space=pltpu.VMEM),
        scratch_shapes=scratch,
        compiler_params=pltpu.CompilerParams(
            collective_id=0, has_side_effects=True, vmem_limit_bytes=56 * 2**20
        ),
    )(*flat)
    result = pl.pallas_call(
        functools.partial(finish, X, Y),
        out_shape=jax.ShapeDtypeStruct((cells, Z), jnp.float32),
        in_specs=[pl.BlockSpec(memory_space=pltpu.VMEM)] * 2,
        out_specs=pl.BlockSpec(memory_space=pltpu.VMEM),
        compiler_params=pltpu.CompilerParams(vmem_limit_bytes=16 * 2**20),
    )(delta, flat[0])
    return result.reshape(X, Y, Z)


def solution(mesh):
    placed = (P("gx", "gy", None), P("gx", "gy", None), P("gx", "gy", None))
    return jax.shard_map(
        per_device, mesh=mesh, in_specs=placed, out_specs=P("gx", "gy", None), check_vma=False
    )
```

profile of v0, /device:TPU:0, one launch (start us, length us, event | category | flops | bytes accessed | tf_op | source)
XLA Modules:
  0.0 28.6 jit_solution(15757854351725158309)
XLA Ops:
  0.0 0.0 copy-start
  0.0 26.0 %shard_map.37.delta = f32[1024,128]{1,0:T(8,128)} custom-call(f32[1024,128]{1,0:T(8,128)} %bitcast.4, f32[1024,128]{1,0:T(8,128)} %bitcast.6, f32[1024,128]{1,0:T(8,128)} %bitcast.7), custom_call_target="tpu_custom_call" | custom-call | tf_op jit(solution)/shard_map/pallas_call | solution.py:516
  26.0 0.0 copy-done
  26.0 0.0 copy-start.1
  26.0 1.0 %copy-done.1 = f32[1024,128]{1,0:T(8,128)S(1)} copy-done((f32[1024,128]{1,0:T(8,128)S(1)}, f32[1024,128]{1,0:T(8,128)}, u32[]{:S(2)}) %copy-start.1) | copy-done | bytes 524312
  27.0 1.5 %shard_map.38 = f32[1024,128]{1,0:T(8,128)} custom-call(f32[1024,128]{1,0:T(8,128)S(1)} %copy-done.1, f32[1024,128]{1,0:T(8,128)S(1)} %bitcast.5), custom_call_target="tpu_custom_call" | custom-call | tf_op jit(solution)/shard_map/pallas_call | solution.py:526
Async XLA Ops:
  0.0 26.0 %copy-start = (f32[32,32,128]{2,1,0:T(8,128)S(1)}, f32[32,32,128]{2,1,0:T(8,128)}, u32[]{:S(2)}) copy-start(f32[32,32,128]{2,1,0:T(8,128)} %param.3) | copy-start | bytes 1572868
  26.0 1.0 %copy-start.1 = (f32[1024,128]{1,0:T(8,128)S(1)}, f32[1024,128]{1,0:T(8,128)}, u32[]{:S(2)}) copy-start(f32[1024,128]{1,0:T(8,128)} %shard_map.37.delta) | copy-start | bytes 1572868
where the time goes:
time: 28.8 us; the launch traced here: 28.6 us
  Pallas kernels  27.5 us (95%)
  local copies, waits for them, and re-layouts  1.04 us (4%)
    pallas_call x1, Pallas kernels, per_device(): pl.pallas_call(functools.partial(kernel, X, Y), out_shape=jax.ShapeDtypeS...  26 us
    pallas_call x1, Pallas kernels, per_device(): pl.pallas_call(functools.partial(finish, X, Y), out_shape=jax.ShapeDtypeS...  1.54 us
    unnamed x4, local copies, waits for them, and re-layouts  1.04 us

commit v1 on v0

--- a/solution.py
+++ b/solution.py
@@ -73,13 +73,11 @@
         ones = jnp.ones((rows, 128), jnp.float32)
         return blocks(0, half, size, functools.partial(body, False), ((ones, ones), (ones, ones)))
     (_, g_f), (_, g_b) = blocks(half, cells, size, functools.partial(body, True), carry)
-    gains[0] = near[plane(0, rows)]
-    gains[1] = g_b
-    gains[2] = g_f
-    gains[3] = near[plane(cells - 1, rows)]
-
-
-def sweep_values(rhs, links, cells, rows, fwd_p, bwd_p, value, ends):
+    for k, value in enumerate((near[plane(0, rows)], g_b, g_f, near[plane(cells - 1, rows)])):
+        gains.put(k, value)
+
+
+def sweep_values(rhs, links, cells, rows, fwd_p, bwd_p, value, ends, at=0):
     size = 4
 
     def body(keep, i, carry):
@@ -101,8 +99,8 @@
     zeros = jnp.zeros((rows, 128), jnp.float32)
     carry = blocks(0, half, size, functools.partial(body, False), (zeros, zeros))
     y_f, y_b = blocks(half, cells, size, functools.partial(body, True), carry)
-    ends[0] = y_b
-    ends[1] = y_f
+    ends.put(at, y_b)
+    ends.put(at + 1, y_f)
 
 
 def back_substitute(before, after, cells, rows, near, far, value, unroll, store):
@@ -122,133 +120,171 @@
     lax.fori_loop(0, cells // 2 // unroll, lap, (before, after))
 
 
+def remote(src, dst, send, recv, axis, to):
+    return pltpu.make_async_remote_copy(
+        src_ref=src, dst_ref=dst, send_sem=send, recv_sem=recv, device_id={axis: to}, device_id_type=MESH
+    )
+
+
+class Parcel:
+    def __init__(self, system, refs):
+        self.system = system
+        self.stage, self.everyone, self.send_sem, self.recv_sem = refs
+
+    def put(self, k, value):
+        rows = self.system.rows
+        for o in range(self.system.owners):
+            self.stage[o, k] = value[o * rows : (o + 1) * rows]
+
+    def copy(self, o):
+        own = self.system
+        return remote(
+            self.stage.at[o], self.everyone.at[own.me], self.send_sem.at[o], self.recv_sem.at[own.me],
+            own.axis, o * own.stride,
+        )
+
+    def send(self):
+        own = self.system
+        for o in range(own.owners):
+
+            @pl.when(own.me != o * own.stride)
+            def _():
+                self.copy(o).start()
+
+        @pl.when(own.mine)
+        def _():
+            self.everyone[own.me] = self.stage[own.group]
+
+    def arrived(self):
+        own = self.system
+        for d in range(1, own.count):
+            k = lax.rem(own.me + d, own.count)
+            part = self.everyone.at[k]
+            remote(part, part, self.recv_sem.at[k], self.recv_sem.at[k], own.axis, k).wait_recv()
+
+    def drain(self):
+        for o in range(self.system.owners):
+
+            @pl.when(self.system.me != o * self.system.stride)
+            def _():
+                self.copy(o).wait_send()
+
+
 class Reduced:
-    def __init__(self, axis, rows, refs):
+    def __init__(self, axis, rows, merged, refs):
         self.axis, self.count, self.me = axis, lax.axis_size(axis), lax.axis_index(axis)
-        self.owners = min(self.count, rows // ROWS)
-        self.rows = rows // self.owners
+        self.owners, self.rows = groups(self.count, rows)
         self.stride = self.count // self.owners
         self.mine = lax.rem(self.me, self.stride) == 0
         self.group = self.me // self.stride
-        (self.gains, self.ends, self.all_gains, self.all_ends, self.relation, self.reply, self.sides) = refs[:7]
-        (self.gain_send, self.gain_recv, self.end_send, self.end_recv, self.reply_send, self.reply_recv) = refs[7:]
-
-    def copy(self, src, dst, send, recv, to):
-        return pltpu.make_async_remote_copy(
-            src_ref=src, dst_ref=dst, send_sem=send, recv_sem=recv,
-            device_id={self.axis: to}, device_id_type=MESH,
-        )
-
-    def to_owner(self, o, source, everyone, send, recv):
-        return self.copy(
-            source.at[:, pl.ds(o * self.rows, self.rows), :], everyone.at[self.me],
-            send.at[o], recv.at[self.me], o * self.stride,
-        )
-
-    def spread(self, source, everyone, send, recv):
-        for o in range(self.owners):
-
-            @pl.when(self.me != o * self.stride)
-            def _():
-                self.to_owner(o, source, everyone, send, recv).start()
-
-            @pl.when(self.me == o * self.stride)
-            def _():
-                everyone[o * self.stride] = source[:, o * self.rows : (o + 1) * self.rows, :]
-
-    def send_gains(self):
-        self.spread(self.gains, self.all_gains, self.gain_send, self.gain_recv)
-
-    def send_ends(self):
-        self.spread(self.ends, self.all_ends, self.end_send, self.end_recv)
-
-    def arrived(self, everyone, recv):
-        for d in range(1, self.count):
-            k = lax.rem(self.me + d, self.count)
-            self.copy(everyone.at[k], everyone.at[k], recv.at[k], recv.at[k], k).wait_recv()
+        self.merged = merged
+        self.gains = Parcel(self, refs[:4])
+        self.ends = self.gains if merged else Parcel(self, refs[4:8])
+        refs = refs[4 if merged else 8 :]
+        (self.relation, self.reply, self.replies, self.sides) = refs[:4]
+        (self.reply_send, self.reply_recv, self.forward_send, self.forward_recv) = refs[4:]
+        self.shift = 4 if merged else 0
 
     def factor(self):
         @pl.when(self.mine)
         def _():
-            self.arrived(self.all_gains, self.gain_recv)
+            self.gains.arrived()
             gain = jnp.zeros((self.rows, 128), jnp.float32)
             for k in range(self.count):
-                head_west, head_east = self.all_gains[k, 0], self.all_gains[k, 1]
-                tail_west, tail_east = self.all_gains[k, 2], self.all_gains[k, 3]
+                head_west, head_east, tail_west, tail_east = (self.gains.everyone[k, v] for v in range(4))
                 scale = inverse(1.0 - head_west * gain)
                 beta, gamma = head_east * scale, tail_west * gain
                 self.relation[k, 0], self.relation[k, 1] = scale, beta
                 self.relation[k, 2], self.relation[k, 3] = gamma, gain
                 gain = tail_east + gamma * beta
 
-    def reply_copy(self, k):
-        return self.copy(
-            self.reply.at[k], self.sides.at[self.group],
-            self.reply_send.at[k], self.reply_recv.at[self.group], k,
+    def reply_copy(self, o):
+        return remote(
+            self.reply.at[pl.ds(o * self.stride, self.stride)], self.replies.at[self.group],
+            self.reply_send.at[o], self.reply_recv.at[self.group], self.axis, o * self.stride,
+        )
+
+    def forward_copy(self, member):
+        return remote(
+            self.replies.at[:, member], self.sides, self.forward_send.at[member], self.forward_recv,
+            self.axis, self.group * self.stride + member,
         )
 
     def solve(self):
         @pl.when(self.mine)
         def _():
-            self.arrived(self.all_ends, self.end_recv)
+            if not self.merged:
+                self.ends.arrived()
             value = jnp.zeros((self.rows, 128), jnp.float32)
             alphas, values = [], []
             for k in range(self.count):
                 values.append(value)
                 scale, gamma = self.relation[k, 0], self.relation[k, 2]
-                head_west, tail_west = self.all_gains[k, 0], self.all_gains[k, 2]
-                alpha = (self.all_ends[k, 0] + head_west * value) * scale
-                value = (self.all_ends[k, 1] + tail_west * value) + gamma * alpha
+                head_west, tail_west = self.gains.everyone[k, 0], self.gains.everyone[k, 2]
+                alpha = (self.ends.everyone[k, self.shift] + head_west * value) * scale
+                value = (self.ends.everyone[k, self.shift + 1] + tail_west * value) + gamma * alpha
                 alphas.append(alpha)
             after = jnp.zeros((self.rows, 128), jnp.float32)
             for k in reversed(range(self.count)):
                 self.reply[k, 1] = after
                 after = alphas[k] + self.relation[k, 1] * after
                 self.reply[k, 0] = values[k] + self.relation[k, 3] * after
-            for d in range(1, self.count):
-                self.reply_copy(lax.rem(self.me + d, self.count)).start()
-            self.sides[self.group] = self.reply[self.me]
+            for d in range(1, self.owners):
+                self.reply_copy(lax.rem(self.group + d, self.owners)).start()
+            self.replies[self.group] = self.reply[pl.ds(self.me, self.stride)]
 
     def result(self):
-        for o in range(self.owners):
-
-            @pl.when(self.me != o * self.stride)
+        @pl.when(self.mine)
+        def _():
+            for d in range(1, self.owners):
+                o = lax.rem(self.group + d, self.owners)
+                part = self.replies.at[o]
+                remote(
+                    part, part, self.reply_recv.at[o], self.reply_recv.at[o], self.axis, o * self.stride
+                ).wait_recv()
+            for member in range(1, self.stride):
+                self.forward_copy(member).start()
+            self.sides[...] = self.replies[:, 0]
+
+        if self.stride > 1:
+
+            @pl.when(jnp.logical_not(self.mine))
             def _():
-                self.copy(
-                    self.sides.at[o], self.sides.at[o], self.reply_recv.at[o], self.reply_recv.at[o],
-                    o * self.stride,
+                remote(
+                    self.sides, self.sides, self.forward_recv, self.forward_recv,
+                    self.axis, self.group * self.stride,
                 ).wait_recv()
 
         whole = (self.owners * self.rows, 128)
         return self.sides[:, 0].reshape(whole), self.sides[:, 1].reshape(whole)
 
     def drain(self):
-        for o in range(self.owners):
-
-            @pl.when(self.me != o * self.stride)
-            def _():
-                self.to_owner(o, self.gains, self.all_gains, self.gain_send, self.gain_recv).wait_send()
-                self.to_owner(o, self.ends, self.all_ends, self.end_send, self.end_recv).wait_send()
-
         @pl.when(self.mine)
         def _():
-            for d in range(1, self.count):
-                self.reply_copy(lax.rem(self.me + d, self.count)).wait_send()
-
-
-def reduced_scratch(count, rows):
+            for d in range(1, self.owners):
+                self.reply_copy(lax.rem(self.group + d, self.owners)).wait_send()
+            for member in range(1, self.stride):
+                self.forward_copy(member).wait_send()
+
+
+def groups(count, rows):
     owners = min(count, rows // ROWS)
-    part = rows // owners
+    return owners, rows // owners
+
+
+def reduced_scratch(count, rows, merged):
+    owners, part = groups(count, rows)
     dma = pltpu.SemaphoreType.DMA
-    return [
-        pltpu.VMEM((4, rows, 128), jnp.float32),
-        pltpu.VMEM((2, rows, 128), jnp.float32),
-        pltpu.VMEM((count, 4, part, 128), jnp.float32),
-        pltpu.VMEM((count, 2, part, 128), jnp.float32),
-        pltpu.VMEM((count, 4, part, 128), jnp.float32),
-        pltpu.VMEM((count, 2, part, 128), jnp.float32),
-        pltpu.VMEM((owners, 2, part, 128), jnp.float32),
-        dma((owners,)), dma((count,)), dma((owners,)), dma((count,)), dma((count,)), dma((owners,)),
+
+    def vmem(*shape):
+        return pltpu.VMEM(shape + (part, 128), jnp.float32)
+
+    scratch = []
+    for values in (6,) if merged else (4, 2):
+        scratch += [vmem(owners, values), vmem(count, values), dma((owners,)), dma((count,))]
+    return scratch + [
+        vmem(count, 4), vmem(count, 2), vmem(owners, count // owners, 2), vmem(owners, 2),
+        dma((owners,)), dma((owners,)), dma((count // owners,)), dma,
     ]
 
 
@@ -258,8 +294,8 @@
     (stage_x, stage_y, halo_x, halo_y, halo_send, halo_recv, force, link_x, link_y, link_z) = scratch[:10]
     fwd_x, bwd_x, near_x, far_x, value_x, fwd_y, bwd_y, near_y, far_y, value_y = scratch[10:20]
     first, up_z, piv_z, lag_z, lead_z, val_z, low_z, h, c, q, load_sem = scratch[20:31]
-    along_x = Reduced("gx", Y, scratch[31:44])
-    along_y = Reduced("gy", X, scratch[44:57])
+    along_x = Reduced("gx", Y, True, scratch[31:43])
+    along_y = Reduced("gy", X, False, scratch[43:59])
     nx, ny, me_x, me_y = along_x.count, along_y.count, along_x.me, along_y.me
 
     part = X * Y // PARTS
@@ -377,16 +413,24 @@
 
     segment_x = (link_x, X, Y, fwd_x, bwd_x, near_x, far_x, along_x.gains)
     factor_segment(*segment_x, factor_segment(*segment_x))
-    along_x.send_gains()
-    sweep_values(force, link_x, X, Y, fwd_x, bwd_x, value_x, along_x.ends)
-    along_x.send_ends()
+    sweep_values(force, link_x, X, Y, fwd_x, bwd_x, value_x, along_x.gains, 4)
+    along_x.gains.send()
 
     segment_y = (link_y, Y, X, fwd_y, bwd_y, near_y, far_y, along_y.gains)
+    factor_segment(*segment_y, factor_segment(*segment_y))
+    along_y.gains.send()
+
     along_x.factor()
-    halfway = factor_segment(*segment_y)
     along_x.solve()
-    factor_segment(*segment_y, halfway)
-    along_y.send_gains()
+
+    def turn_links(k, carry):
+        for u in range(2):
+            up_z[pl.ds(chunks + k + u, Z, stride=chunks), :] = link_z[plane(k + u, 128)].T
+        return carry
+
+    ones, zeros = (jnp.full((chunks, 128), v, jnp.float32) for v in (1.0, 0.0))
+    up_z[plane(0, chunks)] = zeros
+    blocks(0, chunks, 2, turn_links, 0)
 
     before, after = along_x.result()
 
@@ -399,17 +443,12 @@
     back_substitute(before, after, X, Y, near_x, far_x, value_x, 4, store_first)
 
     sweep_values(first, link_y, Y, X, fwd_y, bwd_y, value_y, along_y.ends)
-    along_y.send_ends()
+    along_y.ends.send()
     along_y.factor()
-
-    def turn_links(k, carry):
-        for u in range(2):
-            up_z[pl.ds(chunks + k + u, Z, stride=chunks), :] = link_z[plane(k + u, 128)].T
-        return carry
-
-    ones, zeros = (jnp.full((chunks, 128), v, jnp.float32) for v in (1.0, 0.0))
-    up_z[plane(0, chunks)] = zeros
-    blocks(0, chunks, 2, turn_links, 0)
+    along_x.gains.drain()
+    along_y.gains.drain()
+    along_x.drain()
+
     half = Z // 2
 
     def factor_z(i, carry):
@@ -429,6 +468,12 @@
     carry = blocks(0, half // 2, 8, factor_z, (ones, ones))
     along_y.solve()
     s_f, s_b = blocks(half // 2, half, 8, factor_z, carry)
+    along_y.ends.drain()
+    for inside, send, _ in halos:
+
+        @pl.when(inside)
+        def _():
+            send.wait_send()
     middle = inverse(s_f + s_b * lead_z[plane(half - 1, chunks)])
     before, after = along_y.result()
     per_chunk = 128 // X
@@ -470,14 +515,8 @@
 
     blocks(0, half, 8, back_z, (below, above))
 
-    for inside, send, _ in halos:
-
-        @pl.when(inside)
-        def _():
-            send.wait_send()
-
-    along_x.drain()
     along_y.drain()
+
 
 def finish(X, Y, delta, h, out):
     chunks, per_chunk = X * Y // 128, 128 // X
@@ -511,7 +550,7 @@
         vmem(cells, Z), vmem(cells + Y, Z), vmem(cells + X, Z), vmem(cells, Z),
     ]
     scratch += [vmem(cells, Z) for _ in range(11)] + [vmem(cells + chunks, Z)] + [vmem(cells, Z) for _ in range(8)] + [pltpu.SemaphoreType.DMA((3, PARTS))]
-    scratch += reduced_scratch(nx, Y) + reduced_scratch(ny, X)
+    scratch += reduced_scratch(nx, Y, True) + reduced_scratch(ny, X, False)
     flat = [array.reshape(cells, Z) for array in (water_head, conductivity, recharge)]
     delta = pl.pallas_call(
         functools.partial(kernel, X, Y),

time: 28.8 us -> 29.1 us (1.010)
  Pallas kernels: 27.5 us -> 27.8 us
    pallas_call x1, Pallas kernels: 26 us -> 26.3 us  [per_device(): pl.pallas_call(functools.partial(kernel, X, Y), out_shape=jax.ShapeDtypeS...]
where the time goes in v1:
time: 29.1 us; the launch traced here: 28.9 us
  Pallas kernels  27.8 us (96%)
  local copies, waits for them, and re-layouts  1.04 us (4%)
    pallas_call x1, Pallas kernels, per_device(): pl.pallas_call(functools.partial(kernel, X, Y), out_shape=jax.ShapeDtypeS...  26.3 us
    pallas_call x1, Pallas kernels, per_device(): pl.pallas_call(functools.partial(finish, X, Y), out_shape=jax.ShapeDtypeS...  1.54 us
    unnamed x4, local copies, waits for them, and re-layouts  1.04 us

profile of v1, /device:TPU:0, one launch (start us, length us, event | category | flops | bytes accessed | tf_op | source)
XLA Modules:
  0.0 28.9 jit_solution(10104437188318770944)
XLA Ops:
  0.0 0.0 copy-start
  0.0 26.3 %shard_map.37.delta = f32[1024,128]{1,0:T(8,128)} custom-call(f32[1024,128]{1,0:T(8,128)} %bitcast.4, f32[1024,128]{1,0:T(8,128)} %bitcast.6, f32[1024,128]{1,0:T(8,128)} %bitcast.7), custom_call_target="tpu_custom_call" | custom-call | tf_op jit(solution)/shard_map/pallas_call | solution.py:555
  26.3 0.0 copy-done
  26.3 0.0 copy-start.1
  26.3 1.0 %copy-done.1 = f32[1024,128]{1,0:T(8,128)S(1)} copy-done((f32[1024,128]{1,0:T(8,128)S(1)}, f32[1024,128]{1,0:T(8,128)}, u32[]{:S(2)}) %copy-start.1) | copy-done | bytes 524312
  27.4 1.5 %shard_map.38 = f32[1024,128]{1,0:T(8,128)} custom-call(f32[1024,128]{1,0:T(8,128)S(1)} %copy-done.1, f32[1024,128]{1,0:T(8,128)S(1)} %bitcast.5), custom_call_target="tpu_custom_call" | custom-call | tf_op jit(solution)/shard_map/pallas_call | solution.py:565
Async XLA Ops:
  0.0 26.3 %copy-start = (f32[32,32,128]{2,1,0:T(8,128)S(1)}, f32[32,32,128]{2,1,0:T(8,128)}, u32[]{:S(2)}) copy-start(f32[32,32,128]{2,1,0:T(8,128)} %param.3) | copy-start | bytes 1572868
  26.3 1.0 %copy-start.1 = (f32[1024,128]{1,0:T(8,128)S(1)}, f32[1024,128]{1,0:T(8,128)}, u32[]{:S(2)}) copy-start(f32[1024,128]{1,0:T(8,128)} %shard_map.37.delta) | copy-start | bytes 1572868

commit v2 on v1

--- a/solution.py
+++ b/solution.py
@@ -267,6 +267,83 @@
                 self.forward_copy(member).wait_send()
 
 
+class Everywhere:
+    def __init__(self, axis, refs):
+        self.axis, self.count, self.me = axis, lax.axis_size(axis), lax.axis_index(axis)
+        self.relation = refs[8]
+        self.gains, self.ends = (Broadcast(self, refs[4 * k : 4 * k + 4]) for k in range(2))
+
+    def factor(self):
+        self.gains.arrived()
+        gain = jnp.zeros(self.relation.shape[2:], jnp.float32)
+        for k in range(self.count):
+            head_west, head_east, tail_west, tail_east = (self.gains.everyone[k, v] for v in range(4))
+            scale = inverse(1.0 - head_west * gain)
+            beta, gamma = head_east * scale, tail_west * gain
+            self.relation[k, 0], self.relation[k, 1] = scale, beta
+            self.relation[k, 2], self.relation[k, 3] = gamma, gain
+            gain = tail_east + gamma * beta
+
+    def solve(self):
+        self.ends.arrived()
+        zeros = jnp.zeros(self.relation.shape[2:], jnp.float32)
+        value, alphas, values = zeros, [], []
+        for k in range(self.count):
+            values.append(value)
+            alpha = (self.ends.everyone[k, 0] + self.gains.everyone[k, 0] * value) * self.relation[k, 0]
+            value = (self.ends.everyone[k, 1] + self.gains.everyone[k, 2] * value) + self.relation[k, 2] * alpha
+            alphas.append(alpha)
+        after, mine_before, mine_after = zeros, zeros, zeros
+        for k in reversed(range(self.count)):
+            here = self.me == k
+            mine_after = jnp.where(here, after, mine_after)
+            after = alphas[k] + self.relation[k, 1] * after
+            mine_before = jnp.where(here, values[k] + self.relation[k, 3] * after, mine_before)
+        return mine_before, mine_after
+
+
+class Broadcast:
+    def __init__(self, system, refs):
+        self.system = system
+        self.stage, self.everyone, self.send_sem, self.recv_sem = refs
+
+    def put(self, k, value):
+        self.stage[k] = value
+
+    def copies(self):
+        own = self.system
+        for d in range(1, own.count):
+            to = lax.rem(own.me + d, own.count)
+            yield remote(
+                self.stage, self.everyone.at[own.me], self.send_sem.at[to], self.recv_sem.at[own.me], own.axis, to
+            )
+
+    def send(self):
+        for copy in self.copies():
+            copy.start()
+        self.everyone[self.system.me] = self.stage[...]
+
+    def arrived(self):
+        own = self.system
+        for d in range(1, own.count):
+            k = lax.rem(own.me + d, own.count)
+            part = self.everyone.at[k]
+            remote(part, part, self.recv_sem.at[k], self.recv_sem.at[k], own.axis, k).wait_recv()
+
+    def drain(self):
+        for copy in self.copies():
+            copy.wait_send()
+
+
+def everywhere_scratch(count, rows):
+    dma = pltpu.SemaphoreType.DMA((count,))
+
+    def vmem(*shape):
+        return pltpu.VMEM(shape + (rows, 128), jnp.float32)
+
+    return [vmem(4), vmem(count, 4), dma, dma, vmem(2), vmem(count, 2), dma, dma, vmem(count, 4)]
+
+
 def groups(count, rows):
     owners = min(count, rows // ROWS)
     return owners, rows // owners
@@ -294,8 +371,8 @@
     (stage_x, stage_y, halo_x, halo_y, halo_send, halo_recv, force, link_x, link_y, link_z) = scratch[:10]
     fwd_x, bwd_x, near_x, far_x, value_x, fwd_y, bwd_y, near_y, far_y, value_y = scratch[10:20]
     first, up_z, piv_z, lag_z, lead_z, val_z, low_z, h, c, q, load_sem = scratch[20:31]
-    along_x = Reduced("gx", Y, True, scratch[31:43])
-    along_y = Reduced("gy", X, False, scratch[43:59])
+    along_x = Reduced("gx", Y, False, scratch[31:47])
+    along_y = Everywhere("gy", scratch[47:56])
     nx, ny, me_x, me_y = along_x.count, along_y.count, along_x.me, along_y.me
 
     part = X * Y // PARTS
@@ -413,24 +490,16 @@
 
     segment_x = (link_x, X, Y, fwd_x, bwd_x, near_x, far_x, along_x.gains)
     factor_segment(*segment_x, factor_segment(*segment_x))
-    sweep_values(force, link_x, X, Y, fwd_x, bwd_x, value_x, along_x.gains, 4)
     along_x.gains.send()
+    sweep_values(force, link_x, X, Y, fwd_x, bwd_x, value_x, along_x.ends)
+    along_x.ends.send()
 
     segment_y = (link_y, Y, X, fwd_y, bwd_y, near_y, far_y, along_y.gains)
-    factor_segment(*segment_y, factor_segment(*segment_y))
+    along_x.factor()
+    halfway = factor_segment(*segment_y)
+    along_x.solve()
+    factor_segment(*segment_y, halfway)
     along_y.gains.send()
-
-    along_x.factor()
-    along_x.solve()
-
-    def turn_links(k, carry):
-        for u in range(2):
-            up_z[pl.ds(chunks + k + u, Z, stride=chunks), :] = link_z[plane(k + u, 128)].T
-        return carry
-
-    ones, zeros = (jnp.full((chunks, 128), v, jnp.float32) for v in (1.0, 0.0))
-    up_z[plane(0, chunks)] = zeros
-    blocks(0, chunks, 2, turn_links, 0)
 
     before, after = along_x.result()
 
@@ -445,9 +514,15 @@
     sweep_values(first, link_y, Y, X, fwd_y, bwd_y, value_y, along_y.ends)
     along_y.ends.send()
     along_y.factor()
-    along_x.gains.drain()
-    along_y.gains.drain()
-    along_x.drain()
+
+    def turn_links(k, carry):
+        for u in range(2):
+            up_z[pl.ds(chunks + k + u, Z, stride=chunks), :] = link_z[plane(k + u, 128)].T
+        return carry
+
+    ones, zeros = (jnp.full((chunks, 128), v, jnp.float32) for v in (1.0, 0.0))
+    up_z[plane(0, chunks)] = zeros
+    blocks(0, chunks, 2, turn_links, 0)
 
     half = Z // 2
 
@@ -465,17 +540,20 @@
             ref[at] = value
         return tuple(states)
 
-    carry = blocks(0, half // 2, 8, factor_z, (ones, ones))
-    along_y.solve()
-    s_f, s_b = blocks(half // 2, half, 8, factor_z, carry)
-    along_y.ends.drain()
+    s_f, s_b = blocks(0, half, 8, factor_z, (ones, ones))
+    middle = inverse(s_f + s_b * lead_z[plane(half - 1, chunks)])
+
+    for system in (along_x, along_y):
+        system.gains.drain()
+    along_x.ends.drain()
+    along_x.drain()
     for inside, send, _ in halos:
 
         @pl.when(inside)
         def _():
             send.wait_send()
-    middle = inverse(s_f + s_b * lead_z[plane(half - 1, chunks)])
-    before, after = along_y.result()
+
+    before, after = along_y.solve()
     per_chunk = 128 // X
 
     def store_second(block, lows, highs):
@@ -515,7 +593,7 @@
 
     blocks(0, half, 8, back_z, (below, above))
 
-    along_y.drain()
+    along_y.ends.drain()
 
 
 def finish(X, Y, delta, h, out):
@@ -550,7 +628,7 @@
         vmem(cells, Z), vmem(cells + Y, Z), vmem(cells + X, Z), vmem(cells, Z),
     ]
     scratch += [vmem(cells, Z) for _ in range(11)] + [vmem(cells + chunks, Z)] + [vmem(cells, Z) for _ in range(8)] + [pltpu.SemaphoreType.DMA((3, PARTS))]
-    scratch += reduced_scratch(nx, Y, True) + reduced_scratch(ny, X, False)
+    scratch += reduced_scratch(nx, Y, False) + everywhere_scratch(ny, X)
     flat = [array.reshape(cells, Z) for array in (water_head, conductivity, recharge)]
     delta = pl.pallas_call(
         functools.partial(kernel, X, Y),

time: 29.1 us -> 26.8 us (0.921)
  Pallas kernels: 27.8 us -> 25.6 us
    pallas_call x1, Pallas kernels: 26.3 us -> 24 us  [per_device(): pl.pallas_call(functools.partial(kernel, X, Y), out_shape=jax.ShapeDtypeS...]
where the time goes in v2:
time: 26.8 us; the launch traced here: 26.6 us
  Pallas kernels  25.6 us (96%)
  local copies, waits for them, and re-layouts  1.04 us (4%)
    pallas_call x1, Pallas kernels, per_device(): pl.pallas_call(functools.partial(kernel, X, Y), out_shape=jax.ShapeDtypeS...  24 us
    pallas_call x1, Pallas kernels, per_device(): pl.pallas_call(functools.partial(finish, X, Y), out_shape=jax.ShapeDtypeS...  1.54 us
    unnamed x4, local copies, waits for them, and re-layouts  1.04 us

profile of v2, /device:TPU:0, one launch (start us, length us, event | category | flops | bytes accessed | tf_op | source)
XLA Modules:
  0.0 26.6 jit_solution(2488970781786802843)
XLA Ops:
  0.0 0.0 copy-start
  0.0 24.0 %shard_map.37.delta = f32[1024,128]{1,0:T(8,128)} custom-call(f32[1024,128]{1,0:T(8,128)} %bitcast.4, f32[1024,128]{1,0:T(8,128)} %bitcast.6, f32[1024,128]{1,0:T(8,128)} %bitcast.7), custom_call_target="tpu_custom_call" | custom-call | tf_op jit(solution)/shard_map/pallas_call | solution.py:633
  24.1 0.0 copy-done
  24.1 0.0 copy-start.1
  24.1 1.0 %copy-done.1 = f32[1024,128]{1,0:T(8,128)S(1)} copy-done((f32[1024,128]{1,0:T(8,128)S(1)}, f32[1024,128]{1,0:T(8,128)}, u32[]{:S(2)}) %copy-start.1) | copy-done | bytes 524312
  25.1 1.5 %shard_map.38 = f32[1024,128]{1,0:T(8,128)} custom-call(f32[1024,128]{1,0:T(8,128)S(1)} %copy-done.1, f32[1024,128]{1,0:T(8,128)S(1)} %bitcast.5), custom_call_target="tpu_custom_call" | custom-call | tf_op jit(solution)/shard_map/pallas_call | solution.py:643
Async XLA Ops:
  0.0 24.1 %copy-start = (f32[32,32,128]{2,1,0:T(8,128)S(1)}, f32[32,32,128]{2,1,0:T(8,128)}, u32[]{:S(2)}) copy-start(f32[32,32,128]{2,1,0:T(8,128)} %param.3) | copy-start | bytes 1572868
  24.1 1.0 %copy-start.1 = (f32[1024,128]{1,0:T(8,128)S(1)}, f32[1024,128]{1,0:T(8,128)}, u32[]{:S(2)}) copy-start(f32[1024,128]{1,0:T(8,128)} %shard_map.37.delta) | copy-start | bytes 1572868

commit v3 on v2

--- a/solution.py
+++ b/solution.py
@@ -181,8 +181,7 @@
         self.gains = Parcel(self, refs[:4])
         self.ends = self.gains if merged else Parcel(self, refs[4:8])
         refs = refs[4 if merged else 8 :]
-        (self.relation, self.reply, self.replies, self.sides) = refs[:4]
-        (self.reply_send, self.reply_recv, self.forward_send, self.forward_recv) = refs[4:]
+        self.relation, self.reply, self.sides, self.reply_send, self.reply_recv = refs
         self.shift = 4 if merged else 0
 
     def factor(self):
@@ -198,17 +197,14 @@
                 self.relation[k, 2], self.relation[k, 3] = gamma, gain
                 gain = tail_east + gamma * beta
 
-    def reply_copy(self, o):
-        return remote(
-            self.reply.at[pl.ds(o * self.stride, self.stride)], self.replies.at[self.group],
-            self.reply_send.at[o], self.reply_recv.at[self.group], self.axis, o * self.stride,
-        )
-
-    def forward_copy(self, member):
-        return remote(
-            self.replies.at[:, member], self.sides, self.forward_send.at[member], self.forward_recv,
-            self.axis, self.group * self.stride + member,
-        )
+    def reply_copies(self):
+        for member in range(self.stride):
+            for d in range(1 if member == 0 else 0, self.owners):
+                k = lax.rem(self.group + d, self.owners) * self.stride + member
+                yield remote(
+                    self.reply.at[k], self.sides.at[self.group],
+                    self.reply_send.at[k], self.reply_recv.at[self.group], self.axis, k,
+                )
 
     def solve(self):
         @pl.when(self.mine)
@@ -229,31 +225,19 @@
                 self.reply[k, 1] = after
                 after = alphas[k] + self.relation[k, 1] * after
                 self.reply[k, 0] = values[k] + self.relation[k, 3] * after
-            for d in range(1, self.owners):
-                self.reply_copy(lax.rem(self.group + d, self.owners)).start()
-            self.replies[self.group] = self.reply[pl.ds(self.me, self.stride)]
+            for copy in self.reply_copies():
+                copy.start()
+            self.sides[self.group] = self.reply[self.me]
 
     def result(self):
-        @pl.when(self.mine)
-        def _():
-            for d in range(1, self.owners):
-                o = lax.rem(self.group + d, self.owners)
-                part = self.replies.at[o]
+        for o in range(self.owners):
+
+            @pl.when(self.me != o * self.stride)
+            def _():
+                part = self.sides.at[o]
                 remote(
                     part, part, self.reply_recv.at[o], self.reply_recv.at[o], self.axis, o * self.stride
                 ).wait_recv()
-            for member in range(1, self.stride):
-                self.forward_copy(member).start()
-            self.sides[...] = self.replies[:, 0]
-
-        if self.stride > 1:
-
-            @pl.when(jnp.logical_not(self.mine))
-            def _():
-                remote(
-                    self.sides, self.sides, self.forward_recv, self.forward_recv,
-                    self.axis, self.group * self.stride,
-                ).wait_recv()
 
         whole = (self.owners * self.rows, 128)
         return self.sides[:, 0].reshape(whole), self.sides[:, 1].reshape(whole)
@@ -261,10 +245,8 @@
     def drain(self):
         @pl.when(self.mine)
         def _():
-            for d in range(1, self.owners):
-                self.reply_copy(lax.rem(self.group + d, self.owners)).wait_send()
-            for member in range(1, self.stride):
-                self.forward_copy(member).wait_send()
+            for copy in self.reply_copies():
+                copy.wait_send()
 
 
 class Everywhere:
@@ -360,8 +342,7 @@
     for values in (6,) if merged else (4, 2):
         scratch += [vmem(owners, values), vmem(count, values), dma((owners,)), dma((count,))]
     return scratch + [
-        vmem(count, 4), vmem(count, 2), vmem(owners, count // owners, 2), vmem(owners, 2),
-        dma((owners,)), dma((owners,)), dma((count // owners,)), dma,
+        vmem(count, 4), vmem(count, 2), vmem(owners, 2), dma((count,)), dma((owners,)),
     ]
 
 
@@ -370,9 +351,9 @@
     chunks = X * Y // 128
     (stage_x, stage_y, halo_x, halo_y, halo_send, halo_recv, force, link_x, link_y, link_z) = scratch[:10]
     fwd_x, bwd_x, near_x, far_x, value_x, fwd_y, bwd_y, near_y, far_y, value_y = scratch[10:20]
-    first, up_z, piv_z, lag_z, lead_z, val_z, low_z, h, c, q, load_sem = scratch[20:31]
-    along_x = Reduced("gx", Y, False, scratch[31:47])
-    along_y = Everywhere("gy", scratch[47:56])
+    first, up_z, piv_z, lag_z, lead_z, val_z, low_z, h, c, q, load_sem, delta, delta_sem = scratch[20:33]
+    along_x = Reduced("gx", Y, False, scratch[33:46])
+    along_y = Everywhere("gy", scratch[46:55])
     nx, ny, me_x, me_y = along_x.count, along_y.count, along_x.me, along_y.me
 
     part = X * Y // PARTS
@@ -588,12 +569,24 @@
             low = low_z[nearer] + lead_z[nearer] * low
             high = low_z[farther] + lead_z[farther] * high
         for at, value in stores:
-            out[at] = value
+            delta[at] = value
         return low, high
 
-    blocks(0, half, 8, back_z, (below, above))
+    def give(k, start, stop):
+        cells = pl.ds(start * chunks, (stop - start) * chunks)
+        return pltpu.make_async_copy(delta.at[cells], out.at[cells], delta_sem.at[k])
+
+    quarter = half // 2
+    gives = [give(0, quarter, Z - quarter), give(1, 0, quarter), give(2, Z - quarter, Z)]
+    carry = blocks(0, quarter, 8, back_z, (below, above))
+    gives[0].start()
+    blocks(quarter, half, 8, back_z, carry)
+    gives[1].start()
+    gives[2].start()
 
     along_y.ends.drain()
+    for copy in gives:
+        copy.wait()
 
 
 def finish(X, Y, delta, h, out):
@@ -627,14 +620,14 @@
         pltpu.SemaphoreType.DMA((4,)), pltpu.SemaphoreType.DMA((4,)),
         vmem(cells, Z), vmem(cells + Y, Z), vmem(cells + X, Z), vmem(cells, Z),
     ]
-    scratch += [vmem(cells, Z) for _ in range(11)] + [vmem(cells + chunks, Z)] + [vmem(cells, Z) for _ in range(8)] + [pltpu.SemaphoreType.DMA((3, PARTS))]
+    scratch += [vmem(cells, Z) for _ in range(11)] + [vmem(cells + chunks, Z)] + [vmem(cells, Z) for _ in range(8)] + [pltpu.SemaphoreType.DMA((3, PARTS)), vmem(cells, Z), pltpu.SemaphoreType.DMA((3,))]
     scratch += reduced_scratch(nx, Y, False) + everywhere_scratch(ny, X)
     flat = [array.reshape(cells, Z) for array in (water_head, conductivity, recharge)]
     delta = pl.pallas_call(
         functools.partial(kernel, X, Y),
         out_shape=jax.ShapeDtypeStruct((cells, Z), jnp.float32),
         in_specs=[pl.BlockSpec(memory_space=pl.ANY)] * 3,
-        out_specs=pl.BlockSpec(memory_space=pltpu.VMEM),
+        out_specs=pl.BlockSpec(memory_space=pl.ANY),
         scratch_shapes=scratch,
         compiler_params=pltpu.CompilerParams(
             collective_id=0, has_side_effects=True, vmem_limit_bytes=56 * 2**20

time: 26.8 us -> 26.2 us (0.978)
  Pallas kernels: 25.6 us -> 25 us
    pallas_call x1, Pallas kernels: 24 us -> 23.4 us  [per_device(): pl.pallas_call(functools.partial(kernel, X, Y), out_shape=jax.ShapeDtypeS...]
where the time goes in v3:
time: 26.2 us; the launch traced here: 26 us
  Pallas kernels  25 us (95%)
  local copies, waits for them, and re-layouts  1.04 us (4%)
    pallas_call x1, Pallas kernels, per_device(): pl.pallas_call(functools.partial(kernel, X, Y), out_shape=jax.ShapeDtypeS...  23.4 us
    pallas_call x1, Pallas kernels, per_device(): pl.pallas_call(functools.partial(finish, X, Y), out_shape=jax.ShapeDtypeS...  1.54 us
    unnamed x4, local copies, waits for them, and re-layouts  1.04 us

profile of v3, /device:TPU:0, one launch (start us, length us, event | category | flops | bytes accessed | tf_op | source)
XLA Modules:
  0.0 26.0 jit_solution(8785445707624017688)
XLA Ops:
  0.0 0.0 copy-start
  0.0 23.4 %shard_map.37.delta = f32[1024,128]{1,0:T(8,128)} custom-call(f32[1024,128]{1,0:T(8,128)} %bitcast.4, f32[1024,128]{1,0:T(8,128)} %bitcast.6, f32[1024,128]{1,0:T(8,128)} %bitcast.7), custom_call_target="tpu_custom_call" | custom-call | tf_op jit(solution)/shard_map/pallas_call | solution.py:626
  23.4 0.0 copy-done
  23.4 0.0 copy-start.1
  23.5 1.0 %copy-done.1 = f32[1024,128]{1,0:T(8,128)S(1)} copy-done((f32[1024,128]{1,0:T(8,128)S(1)}, f32[1024,128]{1,0:T(8,128)}, u32[]{:S(2)}) %copy-start.1) | copy-done | bytes 524312
  24.5 1.5 %shard_map.38 = f32[1024,128]{1,0:T(8,128)} custom-call(f32[1024,128]{1,0:T(8,128)S(1)} %copy-done.1, f32[1024,128]{1,0:T(8,128)S(1)} %bitcast.5), custom_call_target="tpu_custom_call" | custom-call | tf_op jit(solution)/shard_map/pallas_call | solution.py:636
Async XLA Ops:
  0.0 23.4 %copy-start = (f32[32,32,128]{2,1,0:T(8,128)S(1)}, f32[32,32,128]{2,1,0:T(8,128)}, u32[]{:S(2)}) copy-start(f32[32,32,128]{2,1,0:T(8,128)} %param.3) | copy-start | bytes 1572868
  23.4 1.0 %copy-start.1 = (f32[1024,128]{1,0:T(8,128)S(1)}, f32[1024,128]{1,0:T(8,128)}, u32[]{:S(2)}) copy-start(f32[1024,128]{1,0:T(8,128)} %shard_map.37.delta) | copy-start | bytes 1572868

commit v4 on v3

--- a/solution.py
+++ b/solution.py
@@ -476,8 +476,8 @@
     along_x.ends.send()
 
     segment_y = (link_y, Y, X, fwd_y, bwd_y, near_y, far_y, along_y.gains)
+    halfway = factor_segment(*segment_y)
     along_x.factor()
-    halfway = factor_segment(*segment_y)
     along_x.solve()
     factor_segment(*segment_y, halfway)
     along_y.gains.send()

time: 26.2 us -> 26.1 us (level)
  no operation moved by 1% of the time
where the time goes in v4:
time: 26.1 us; the launch traced here: 25.9 us
  Pallas kernels  24.8 us (95%)
  local copies, waits for them, and re-layouts  1.04 us (4%)
    pallas_call x1, Pallas kernels, per_device(): pl.pallas_call(functools.partial(kernel, X, Y), out_shape=jax.ShapeDtypeS...  23.3 us
    pallas_call x1, Pallas kernels, per_device(): pl.pallas_call(functools.partial(finish, X, Y), out_shape=jax.ShapeDtypeS...  1.54 us
    unnamed x4, local copies, waits for them, and re-layouts  1.04 us

profile of v4, /device:TPU:0, one launch (start us, length us, event | category | flops | bytes accessed | tf_op | source)
XLA Modules:
  0.0 25.9 jit_solution(10425954576527270877)
XLA Ops:
  0.0 0.0 copy-start
  0.0 23.3 %shard_map.37.delta = f32[1024,128]{1,0:T(8,128)} custom-call(f32[1024,128]{1,0:T(8,128)} %bitcast.4, f32[1024,128]{1,0:T(8,128)} %bitcast.6, f32[1024,128]{1,0:T(8,128)} %bitcast.7), custom_call_target="tpu_custom_call" | custom-call | tf_op jit(solution)/shard_map/pallas_call | solution.py:626
  23.3 0.0 copy-done
  23.3 0.0 copy-start.1
  23.3 1.0 %copy-done.1 = f32[1024,128]{1,0:T(8,128)S(1)} copy-done((f32[1024,128]{1,0:T(8,128)S(1)}, f32[1024,128]{1,0:T(8,128)}, u32[]{:S(2)}) %copy-start.1) | copy-done | bytes 524312
  24.4 1.5 %shard_map.38 = f32[1024,128]{1,0:T(8,128)} custom-call(f32[1024,128]{1,0:T(8,128)S(1)} %copy-done.1, f32[1024,128]{1,0:T(8,128)S(1)} %bitcast.5), custom_call_target="tpu_custom_call" | custom-call | tf_op jit(solution)/shard_map/pallas_call | solution.py:636
Async XLA Ops:
  0.0 23.3 %copy-start = (f32[32,32,128]{2,1,0:T(8,128)S(1)}, f32[32,32,128]{2,1,0:T(8,128)}, u32[]{:S(2)}) copy-start(f32[32,32,128]{2,1,0:T(8,128)} %param.3) | copy-start | bytes 1572868
  23.3 1.0 %copy-start.1 = (f32[1024,128]{1,0:T(8,128)S(1)}, f32[1024,128]{1,0:T(8,128)}, u32[]{:S(2)}) copy-start(f32[1024,128]{1,0:T(8,128)} %shard_map.37.delta) | copy-start | bytes 1572868
